TPU v7x, 128 devices: a whole 4x4x4 slice. The times are simulated.
128 devices in a mesh: days: 2 (over x_lo), chan: 64 (over z, y, x_hi, core).
Axes of the slice: x: 4 (x_hi: 2, x_lo: 2; x = x_hi * 2 + x_lo), y: 4, z: 4, core: 2. Of those that a mesh axis runs over, the one named last changes fastest.
Arguments:
- spectra: bfloat16 [8, 512, 8192], P('days', None, 'chan'), may hold values from -6 to 6
- sources: int32 [2], replicated, may hold values from 0 to 8191
- offsets: int32 [8192], P('chan'), may hold values from 0 to 4095
Outputs:
- slant: float32 [128, 2, 2, 256], P('chan')
All inputs are finite; a program needn't handle non-finite values.
Results may differ from a plain program's by a relative error of at most 0.0055.
Values may be sent and summed in bfloat16 or wider, within the bound.
No kernel may reach another device: no remote copies, remote signals or barrier semaphores. Data moves between devices by JAX's collectives and lax.ppermute only.
A program may use at most 64 MiB of HBM per device.

v0:
```python
import functools
import math

import jax
import jax.numpy as jnp
import numpy as np
from jax import lax
from jax.experimental import pallas as pl
from jax.experimental.pallas import tpu as pltpu
from jax.sharding import PartitionSpec as P

BINS = 256
LAGS = 512
NSLOW = 128
NSRC = 2
PERIOD = 4096
LANES = 128
FAST = 8
SLOW = NSLOW // FAST
GROUP = 8
GROUPS = BINS // GROUP
BOTH = ("days", "chan")
NT = (((1,), (1,)), ((), ()))


def inverse_table():
    lag = np.arange(LAGS // 2)[:, None]
    freq = np.arange(BINS)[None, :]
    theta = (lag * freq % LAGS) * (2.0 * math.pi / LAGS)
    cosine, sine = np.cos(theta), np.sin(theta)
    sine[0] = 1 - 2 * (freq[0] % 2)
    table = np.concatenate([cosine, sine], 0) / math.sqrt(BINS)
    return table.astype(np.float32).astype(jnp.bfloat16)


def forward_table(scale):
    freq = np.arange(BINS)[:, None]
    lag = np.arange(LAGS // 2)[None, :]
    theta = (freq * lag % LAGS) * (2.0 * math.pi / LAGS)
    table = np.concatenate([np.cos(theta), -np.sin(theta)], 0) * scale
    high = table.astype(np.float32).astype(jnp.bfloat16)
    low = (table - high.astype(np.float64)).astype(np.float32).astype(jnp.bfloat16)
    return np.concatenate([high, low], 0)


def unit_circle(phase):
    quarter = PERIOD // 4
    turn = (phase + quarter // 2) >> 10
    angle = (phase - turn * quarter).astype(jnp.float32) * (2.0 * math.pi / PERIOD)
    square = angle * angle
    cosine = 1.0 + square * (-1 / 2 + square * (1 / 24 + square * (-1 / 720 + square * (1 / 40320))))
    sine = angle * (1.0 + square * (-1 / 6 + square * (1 / 120 + square * (-1 / 5040 + square * (1 / 362880)))))
    odd = (turn & 1) == 1
    real = jnp.where(odd, sine, cosine)
    imag = jnp.where(odd, cosine, sine)
    real = jnp.where(((turn + 1) & 2) == 2, -real, real)
    imag = jnp.where((turn & 2) == 2, -imag, imag)
    return real, imag


def times(left, right):
    return left[0] * right[0] - left[1] * right[1], left[0] * right[1] + left[1] * right[0]


def front_kernel(
    sources, offsets, spectra, inverse_far, forward_far,
    sent, steep, rotor, held, inverse, forward,
    places, spots, arrived,
):
    windows = spectra.shape[0]
    parts = 2 * BINS // LANES
    block = windows * parts
    peers = sent.shape[0] // block
    pairs = ((offsets, spots), (sources, places), (spectra, held), (inverse_far, inverse), (forward_far, forward))
    copies = [pltpu.make_async_copy(*pair, arrived.at[place]) for place, pair in enumerate(pairs)]
    for copy in copies:
        copy.start()

    copies[0].wait()
    chunk = 32
    for first in range(0, BINS, chunk):
        freq = first + lax.broadcasted_iota(jnp.int32, (chunk, LANES), 0)
        real, imag = unit_circle(freq * spots[...] & (PERIOD - 1))
        rotor[0, first : first + chunk, :] = real
        rotor[1, first : first + chunk, :] = imag
    across = jnp.transpose(jnp.broadcast_to(spots[...].astype(jnp.float32), (LANES, LANES))).astype(jnp.int32)
    table_lane = lax.broadcasted_iota(jnp.int32, (chunk, LANES), 1)

    def place_powers(first):
        turn = across[first : first + chunk] * (table_lane // GROUP * FAST)
        value = unit_circle(turn * (table_lane & (GROUP - 1)) & (PERIOD - 1))
        step = unit_circle(turn * GROUP & (PERIOD - 1))
        for group in range(GROUPS):
            lanes = slice(group % 2 * LANES, (group % 2 + 1) * LANES)
            steep[group // 2, first : first + chunk, lanes] = value[0].astype(jnp.bfloat16)
            steep[group // 2, LANES + first : LANES + first + chunk, lanes] = value[1].astype(jnp.bfloat16)
            if group < GROUPS - 1:
                value = times(value, step)

    place_powers(0)
    place_powers(chunk)
    copies[1].wait()
    row = lax.broadcasted_iota(jnp.int32, (NSRC * block, LANES), 0)
    lane = lax.broadcasted_iota(jnp.int32, (NSRC * block, LANES), 1)
    column = jnp.where(row < block, places[:, 0:1], places[:, 1:2]) - lax.axis_index("chan") * LANES
    hit = jnp.where(lane == column, row & (block - 1), -1)
    copies[2].wait()
    sums = [None] * parts
    for place in range(block):
        window, part = divmod(place, parts)
        chosen = jnp.where(hit == place, 1.0, 0.0).astype(jnp.bfloat16)
        piece = held[window, part * LANES : (part + 1) * LANES, :]
        term = lax.dot_general(chosen, piece, NT, preferred_element_type=jnp.float32)
        sums[part] = term if window == 0 else sums[part] + term
        if place in (block // 2 - 1, block - 1):
            place_powers((2 + place * 2 // block) * chunk)
    total = sums[0]
    for term in sums[1:]:
        total += term
    rounded = total.astype(jnp.bfloat16)
    half = peers // NSRC
    for peer in range(peers):
        source = peer // half
        sent[peer * block : (peer + 1) * block, :] = rounded[source * block : (source + 1) * block]
    copies[3].wait()
    copies[4].wait()


def main_kernel(
    scale,
    received, own, other, steep, rotor, inverse, forward,
    sent,
    cross, analytic, stack, product,
):
    windows = own.shape[0]
    parts = 2 * BINS // LANES
    block = windows * parts
    half = received.shape[0] // block // NSRC
    day = lax.axis_index("days")
    picked = []
    for from_day in (day, 1 - day):
        sums = [None] * 8
        for peer in range(half):
            start = pl.multiple_of((from_day * half + peer) * block, block)
            term = received[pl.ds(start, block), :]
            sums[peer % 8] = term if peer < 8 else sums[peer % 8] + term
        while len(sums) > 1:
            sums = [first + second for first, second in zip(sums[::2], sums[1::2])]
        picked.append(sums[0].astype(jnp.float32))
    columns = jnp.transpose(jnp.concatenate(picked, 0))
    for window in range(2 * windows):
        taken = own if window < windows else other
        inner = window % windows
        for part in range(parts // 2):
            rows = slice(part * LANES, (part + 1) * LANES)
            below = slice(BINS + part * LANES, BINS + (part + 1) * LANES)
            place = window * parts + part
            real_s = jnp.broadcast_to(columns[:, place : place + 1], (LANES, LANES))
            place += parts // 2
            imag_s = jnp.broadcast_to(columns[:, place : place + 1], (LANES, LANES))
            real_x = taken[inner, rows, :].astype(jnp.float32)
            imag_x = taken[inner, below, :].astype(jnp.float32)
            cross[window, rows, :LANES] = (real_s * real_x + imag_s * imag_x).astype(jnp.bfloat16)
            cross[window, rows, LANES:] = (real_s * imag_x - imag_s * real_x).astype(jnp.bfloat16)

    for window in range(2 * windows):
        analytic[window] = jnp.dot(inverse[...], cross[window], preferred_element_type=jnp.float32)
    chunk = 16
    middle = LAGS // 2
    for first in range(0, middle, chunk):
        upper, lower = slice(first, first + chunk), slice(middle + first, middle + first + chunk)
        rising, falling = [None] * 3, [None] * 3
        for window in range(2 * windows):
            cos_re, cos_im = analytic[window, upper, :LANES], analytic[window, upper, LANES:]
            sin_re, sin_im = analytic[window, lower, :LANES], analytic[window, lower, LANES:]
            early = (cos_re - sin_im, cos_im + sin_re)
            late = (cos_re + sin_im, cos_im - sin_re)
            if first == 0:
                edge = lax.broadcasted_iota(jnp.int32, (chunk, LANES), 0) == 0
                early = (jnp.where(edge, cos_re, early[0]), jnp.where(edge, cos_im, early[1]))
                late = (jnp.where(edge, sin_re, late[0]), jnp.where(edge, sin_im, late[1]))
            for sums, (corr, hilb) in ((rising, early), (falling, late)):
                weight = lax.rsqrt(jnp.maximum(corr * corr + hilb * hilb, 0.25))
                for place, term in enumerate((corr, corr * weight, hilb * weight)):
                    sums[place] = term if window == 0 else sums[place] + term
        early, late = (sums[0] * (sums[1] * sums[1] + sums[2] * sums[2]) for sums in (rising, falling))
        if first == 0:
            turning = late[0:1, :] * scale
            late = jnp.where(edge, 0.0, late)
        for rows, weighted in ((upper, early + late), (lower, early - late)):
            large = weighted.astype(jnp.bfloat16)
            stack[rows, :LANES] = large
            stack[rows, LANES:] = (weighted - large.astype(jnp.float32)).astype(jnp.bfloat16)

    value = []
    for first in (0, BINS):
        rows = slice(first, first + BINS)
        wide = jnp.dot(forward[rows, :], stack[rows, :], preferred_element_type=jnp.float32)
        rest = slice(2 * BINS + first, 3 * BINS + first)
        value.append(
            wide[:, :LANES]
            + wide[:, LANES:]
            + jnp.dot(forward[rest, :], stack[rows, :LANES], preferred_element_type=jnp.float32)
        )
    odd = lax.broadcasted_iota(jnp.int32, (BINS, LANES), 0) & 1
    value[0] += jnp.where(odd == 1, -turning, turning)
    side = 2 * FAST * GROUP
    bin_lane = lax.broadcasted_iota(jnp.int32, (8, LANES), 1) & (GROUP - 1)
    spectrum = value
    kept = []
    for pair in range(GROUPS // 2):
        groups = slice(2 * pair, 2 * pair + 2)
        rows = slice(2 * pair * GROUP, 2 * (pair + 1) * GROUP)
        value = (spectrum[0][rows], spectrum[1][rows])
        base = (rotor[0, rows, :], rotor[1, rows, :])
        lines = ([], [])
        for fast in range(FAST):
            for group in range(2):
                bins = slice(group * GROUP, (group + 1) * GROUP)
                real, imag = value[0][bins], value[1][bins]
                left = jnp.concatenate([real, imag], 0).astype(jnp.bfloat16)
                right = jnp.concatenate([-imag, real], 0).astype(jnp.bfloat16)
                lines[group].append(jnp.concatenate([left, right], 1))
            if fast < FAST - 1:
                value = times(value, base)
        both = jnp.concatenate(lines[0] + lines[1], 0)
        both = jnp.dot(both, steep[pair], preferred_element_type=jnp.float32)
        product[2 * pair] = both[:side, :LANES]
        product[2 * pair + 1] = both[side:, LANES:]
        for group in range(2 * pair, 2 * pair + 2):
            tiles = []
            for first in range(0, side, 8 * GROUP):
                tile = product[group, pl.ds(first, 8, stride=GROUP), :]
                for place in range(1, GROUP):
                    line = product[group, pl.ds(first + place, 8, stride=GROUP), :]
                    tile = jnp.where(bin_lane == place, line, tile)
                tiles.append(tile)
            kept.append(jnp.concatenate(tiles, 0))

    spot = lax.broadcasted_iota(jnp.int32, (2 * FAST, LANES), 1) // GROUP
    kept = [pltpu.roll(part, group % SLOW * GROUP, 1) if group % SLOW else part for group, part in enumerate(kept)]
    low_rows = lax.broadcasted_iota(jnp.int32, (8, LANES), 0) < 4
    for slow in range(SLOW):
        halves = []
        for first in (0, SLOW):
            joined = kept[first + -slow % SLOW]
            for place in range(1, SLOW):
                joined = jnp.where(spot == place, kept[first + (place - slow) % SLOW], joined)
            halves.append(pltpu.roll(joined, LANES - slow * GROUP, 1) if slow else joined)
        for pair in range(2):
            left = halves[0][8 * pair : 8 * pair + 8]
            right = halves[1][8 * pair : 8 * pair + 8]
            first = jnp.where(low_rows, left, pltpu.roll(right, 4, 0))
            second = jnp.where(low_rows, pltpu.roll(left, 4, 0), right)
            tile = jnp.concatenate([first, second], 0).astype(jnp.bfloat16)
            for day_side in range(2):
                start = (day_side * half + slow * (FAST // 2) + 2 * pair) * 8
                sent[start : start + 16, :] = tile


def sum_kernel(received, out):
    rows = received.shape[0] // NSRC
    for source in range(NSRC):
        sums = [None] * 8
        for place in range(rows // 16):
            term = received[source * rows + place * 16 : source * rows + (place + 1) * 16, :].astype(jnp.float32)
            sums[place % 8] = term if place < 8 else sums[place % 8] + term
        while len(sums) > 1:
            sums = [first + second for first, second in zip(sums[::2], sums[1::2])]
        total = sums[0][:8] + sums[0][8:]
        for row in range(8):
            upper, slow, part = row // 4, row // 2 % 2, row % 2
            out[slow, source, part, upper * LANES : (upper + 1) * LANES] = total[row]


def in_hbm(array):
    return pltpu.with_memory_space_constraint(array, pltpu.HBM)


def shards(spectra, sources, offsets):
    windows = spectra.shape[0]
    width = spectra.shape[2]
    peers = lax.axis_size("days") * lax.axis_size("chan")
    all_windows = windows * lax.axis_size("days")
    channels = width * lax.axis_size("chan")
    scale = all_windows**1.5 / math.sqrt(channels) / all_windows**3
    scale /= math.sqrt(LAGS)
    forward = forward_table(scale)
    vmem = pl.BlockSpec(memory_space=pltpu.VMEM)
    far = pl.BlockSpec(memory_space=pltpu.HBM)
    block = windows * 2 * BINS // LANES

    other = lax.ppermute(spectra, "days", [(0, 1), (1, 0)])
    inverse = jnp.asarray(inverse_table())
    forward = jnp.asarray(forward)
    candidates, steep, rotor, own, inverse, forward = pl.pallas_call(
        front_kernel,
        out_shape=(
            jax.ShapeDtypeStruct((peers * block, LANES), jnp.bfloat16),
            jax.ShapeDtypeStruct((GROUPS // 2, 2 * LANES, 2 * LANES), jnp.bfloat16),
            jax.ShapeDtypeStruct((2, BINS, LANES), jnp.float32),
            jax.ShapeDtypeStruct(spectra.shape, jnp.bfloat16),
            jax.ShapeDtypeStruct(inverse.shape, jnp.bfloat16),
            jax.ShapeDtypeStruct(forward.shape, jnp.bfloat16),
        ),
        in_specs=[far] * 5,
        out_specs=(vmem,) * 6,
        scratch_shapes=[
            pltpu.VMEM((1, NSRC), jnp.int32),
            pltpu.VMEM((1, width), jnp.int32),
            pltpu.SemaphoreType.DMA((5,)),
        ],
        name="front",
        compiler_params=pltpu.CompilerParams(vmem_limit_bytes=8 << 20),
    )(
        in_hbm(sources.reshape(1, NSRC)),
        in_hbm(offsets.reshape(1, width)),
        in_hbm(spectra),
        in_hbm(inverse),
        in_hbm(forward),
    )
    received = lax.all_to_all(candidates.reshape(peers, block, LANES), BOTH, 0, 0, tiled=True)
    received = received.reshape(peers * block, LANES)
    terms = pl.pallas_call(
        functools.partial(main_kernel, scale),
        out_shape=jax.ShapeDtypeStruct((peers * 8, LANES), jnp.bfloat16),
        in_specs=[vmem] * 7,
        out_specs=vmem,
        scratch_shapes=[
            pltpu.VMEM((all_windows, BINS, 2 * LANES), jnp.bfloat16),
            pltpu.VMEM((all_windows, LAGS, 2 * LANES), jnp.float32),
            pltpu.VMEM((LAGS, 2 * LANES), jnp.bfloat16),
            pltpu.VMEM((GROUPS, 2 * FAST * GROUP, LANES), jnp.float32),
        ],
        name="stack_and_slant",
        compiler_params=pltpu.CompilerParams(vmem_limit_bytes=24 << 20),
    )(received, own, other, steep, rotor, inverse, forward)
    partial = lax.all_to_all(terms.reshape(peers, 8, LANES), BOTH, 0, 0, tiled=True)
    return pl.pallas_call(
        sum_kernel,
        out_shape=jax.ShapeDtypeStruct((NSLOW // lax.axis_size("chan"), NSRC, 2, BINS), jnp.float32),
        in_specs=[vmem],
        out_specs=vmem,
        name="sum",
        compiler_params=pltpu.CompilerParams(vmem_limit_bytes=8 << 20),
    )(partial.reshape(peers * 8, LANES))


def solution(mesh):
    placed = (P("days", None, "chan"), P(), P("chan"))
    return jax.shard_map(
        shards, mesh=mesh, in_specs=placed, out_specs=P("chan", None, None, None), check_vma=False
    )
```

profile of v0, /device:TPU:1, one launch (start us, length us, event | category | flops | bytes accessed | tf_op | source)
XLA Modules:
  0.0 47.3 jit_solution(10995011651075385619)
XLA Ops:
  0.0 2.0 %collective-permute-start = (bf16[4,512,128]{2,1,0:T(8,128)(2,1)}, bf16[4,512,128]{2,1,0:T(8,128)(2,1)S(1)}, u32[]{:S(2)}, u32[]{:S(2)}) collective-permute-start(bf16[4,512,128]{2,1,0:T(8,128)(2,1)} %spectra.1), channel_id=1, source_target_pairs={{0,64},{64,0},{1,65},{65,1},{2,66},{66,2},{3,67},{67,3},{4,68},{68... | collective-permute-start | bytes 1572872 | tf_op jit(solution)/shard_map/ppermute | solution.py:293
  2.0 2.1 %front.1 = (bf16[2048,128]{1,0:T(8,128)(2,1)S(1)}, bf16[16,256,256]{2,1,0:T(8,128)(2,1)S(1)}, f32[2,256,128]{2,1,0:T(8,128)S(1)}, bf16[4,512,128]{2,1,0:T(8,128)...) custom-call(s32[1,2]{1,0:T(1,128)} %bitcast.10, s32[1,128]{1,0:T(1,128)} %bitcast.11, ...), custom_call_target="tpu_custom_call" | custom-call | tf_op jit(solution)/shard_map/front/pallas_call | solution.py:296
  4.2 24.3 %all_to_all.10 = bf16[128,16,128]{2,1,0:T(8,128)(2,1)S(1)} all-to-all(bf16[128,16,128]{2,1,0:T(8,128)(2,1)S(1)} %bitcast.9), channel_id=1, replica_groups=mesh['days'=2,'chan'=64] {'days','chan'}, dimensions={0} | all-to-all | bytes 1048576 | tf_op jit(solution)/shard_map/all_to_all | solution.py:322
  28.5 0.0 collective-permute-done.other
  28.5 3.2 %stack_and_slant.1 = bf16[1024,128]{1,0:T(8,128)(2,1)S(1)} custom-call(bf16[2048,128]{1,0:T(8,128)(2,1)S(1)} %bitcast.6, bf16[4,512,128]{2,1,0:T(8,128)(2,1)S(1)} %get-tuple-element.12.own, bf16[4,512,128]{2,1,0:T(8,128)(2,1)S(1)} %collective-permute-done.other, bf16[16,256,256]{2,1,0:T(8,128)(2,1)S(1)} %get-tuple-element.13.steep, ...), custom_call_target="tpu_custom_call" | custom-call | tf_op jit(solution)/shard_map/stack_and_slant/pallas_call | solution.py:324
  31.7 15.0 %all_to_all.11 = bf16[128,8,128]{2,1,0:T(8,128)(2,1)S(1)} all-to-all(bf16[128,8,128]{2,1,0:T(8,128)(2,1)S(1)} %bitcast.7), channel_id=1, replica_groups=mesh['days'=2,'chan'=64] {'days','chan'}, dimensions={0} | all-to-all | bytes 524288 | tf_op jit(solution)/shard_map/all_to_all | solution.py:338
  46.7 0.6 %sum.1 = f32[2,2,2,256]{3,2,1,0:T(2,128)} custom-call(bf16[1024,128]{1,0:T(8,128)(2,1)S(1)} %bitcast.8), custom_call_target="tpu_custom_call" | custom-call | tf_op jit(solution)/shard_map/sum/pallas_call | solution.py:339
Async XLA Ops:
  0.0 28.5 %collective-permute-start = (bf16[4,512,128]{2,1,0:T(8,128)(2,1)}, bf16[4,512,128]{2,1,0:T(8,128)(2,1)S(1)}, u32[]{:S(2)}, u32[]{:S(2)}) collective-permute-start(bf16[4,512,128]{2,1,0:T(8,128)(2,1)} %spectra.1), channel_id=1, source_target_pairs={{0,64},{64,0},{1,65},{65,1},{2,66},{66,2},{3,67},{67,3},{4,68},{68... | collective-permute-start | bytes 1572872 | tf_op jit(solution)/shard_map/ppermute | solution.py:293
where the time goes:
time: 47.5 us; the launch traced here: 47.3 us
  blocking collectives  39.3 us (83%)
  Pallas kernels  5.97 us (13%)
  starting transfers between devices  2.04 us (4%)
    all_to_all x1, blocking collectives, shards(): lax.all_to_all(candidates.reshape(peers, block, LANES), BOTH, 0, 0, tiled...  24.3 us
    all_to_all x1, blocking collectives, shards(): lax.all_to_all(terms.reshape(peers, 8, LANES), BOTH, 0, 0, tiled=True)  15 us
    pallas_call x1, Pallas kernels, shards(): pl.pallas_call(functools.partial(main_kernel, scale), out_shape=jax.Shape...  3.2 us
    pallas_call x1, Pallas kernels, shards(): pl.pallas_call(front_kernel, out_shape=(jax.ShapeDtypeStruct((peers * blo...  2.12 us
    ppermute x1, starting transfers between devices, shards(): other = lax.ppermute(spectra, 'days', [(0, 1), (1, 0)])  2.04 us
  transfers between devices with their start and end apart: 1, of which 0 were waited for; matrix products, arithmetic and copies ran while one was open for 0% of the time, Pallas kernels for 4%

commit v1 on v0

--- a/solution.py
+++ b/solution.py
@@ -130,7 +130,7 @@
     scale,
     received, own, other, steep, rotor, inverse, forward,
     sent,
-    cross, analytic, stack, product,
+    analytic, stack, product,
 ):
     windows = own.shape[0]
     parts = 2 * BINS // LANES
@@ -151,6 +151,7 @@
     for window in range(2 * windows):
         taken = own if window < windows else other
         inner = window % windows
+        crossed = []
         for part in range(parts // 2):
             rows = slice(part * LANES, (part + 1) * LANES)
             below = slice(BINS + part * LANES, BINS + (part + 1) * LANES)
@@ -160,11 +161,11 @@
             imag_s = jnp.broadcast_to(columns[:, place : place + 1], (LANES, LANES))
             real_x = taken[inner, rows, :].astype(jnp.float32)
             imag_x = taken[inner, below, :].astype(jnp.float32)
-            cross[window, rows, :LANES] = (real_s * real_x + imag_s * imag_x).astype(jnp.bfloat16)
-            cross[window, rows, LANES:] = (real_s * imag_x - imag_s * real_x).astype(jnp.bfloat16)
-
-    for window in range(2 * windows):
-        analytic[window] = jnp.dot(inverse[...], cross[window], preferred_element_type=jnp.float32)
+            real = (real_s * real_x + imag_s * imag_x).astype(jnp.bfloat16)
+            imag = (real_s * imag_x - imag_s * real_x).astype(jnp.bfloat16)
+            crossed.append(jnp.concatenate([real, imag], 1))
+        crossed = jnp.concatenate(crossed, 0)
+        analytic[window] = jnp.dot(inverse[...], crossed, preferred_element_type=jnp.float32)
     chunk = 16
     middle = LAGS // 2
     for first in range(0, middle, chunk):
@@ -327,7 +328,6 @@
         in_specs=[vmem] * 7,
         out_specs=vmem,
         scratch_shapes=[
-            pltpu.VMEM((all_windows, BINS, 2 * LANES), jnp.bfloat16),
             pltpu.VMEM((all_windows, LAGS, 2 * LANES), jnp.float32),
             pltpu.VMEM((LAGS, 2 * LANES), jnp.bfloat16),
             pltpu.VMEM((GROUPS, 2 * FAST * GROUP, LANES), jnp.float32),

time: 47.5 us -> 47.4 us (level)
  no operation moved by 1% of the time
where the time goes in v1:
time: 47.4 us; the launch traced here: 47.2 us
  blocking collectives  39.3 us (83%)
  Pallas kernels  5.84 us (12%)
  starting transfers between devices  2.04 us (4%)
    all_to_all x1, blocking collectives, shards(): lax.all_to_all(candidates.reshape(peers, block, LANES), BOTH, 0, 0, tiled...  24.3 us
    all_to_all x1, blocking collectives, shards(): lax.all_to_all(terms.reshape(peers, 8, LANES), BOTH, 0, 0, tiled=True)  15 us
    pallas_call x1, Pallas kernels, shards(): pl.pallas_call(functools.partial(main_kernel, scale), out_shape=jax.Shape...  3.07 us
    pallas_call x1, Pallas kernels, shards(): pl.pallas_call(front_kernel, out_shape=(jax.ShapeDtypeStruct((peers * blo...  2.12 us
    ppermute x1, starting transfers between devices, shards(): other = lax.ppermute(spectra, 'days', [(0, 1), (1, 0)])  2.04 us
  transfers between devices with their start and end apart: 1, of which 0 were waited for; matrix products, arithmetic and copies ran while one was open for 0% of the time, Pallas kernels for 4%

profile of v1, /device:TPU:1, one launch (start us, length us, event | category | flops | bytes accessed | tf_op | source)
XLA Modules:
  0.0 47.2 jit_solution(13415169327465896288)
XLA Ops:
  0.0 2.0 %collective-permute-start = (bf16[4,512,128]{2,1,0:T(8,128)(2,1)}, bf16[4,512,128]{2,1,0:T(8,128)(2,1)S(1)}, u32[]{:S(2)}, u32[]{:S(2)}) collective-permute-start(bf16[4,512,128]{2,1,0:T(8,128)(2,1)} %spectra.1), channel_id=1, source_target_pairs={{0,64},{64,0},{1,65},{65,1},{2,66},{66,2},{3,67},{67,3},{4,68},{68... | collective-permute-start | bytes 1572872 | tf_op jit(solution)/shard_map/ppermute | solution.py:294
  2.0 2.1 %front.1 = (bf16[2048,128]{1,0:T(8,128)(2,1)S(1)}, bf16[16,256,256]{2,1,0:T(8,128)(2,1)S(1)}, f32[2,256,128]{2,1,0:T(8,128)S(1)}, bf16[4,512,128]{2,1,0:T(8,128)...) custom-call(s32[1,2]{1,0:T(1,128)} %bitcast.10, s32[1,128]{1,0:T(1,128)} %bitcast.11, ...), custom_call_target="tpu_custom_call" | custom-call | tf_op jit(solution)/shard_map/front/pallas_call | solution.py:297
  4.2 24.3 %all_to_all.10 = bf16[128,16,128]{2,1,0:T(8,128)(2,1)S(1)} all-to-all(bf16[128,16,128]{2,1,0:T(8,128)(2,1)S(1)} %bitcast.9), channel_id=1, replica_groups=mesh['days'=2,'chan'=64] {'days','chan'}, dimensions={0} | all-to-all | bytes 1048576 | tf_op jit(solution)/shard_map/all_to_all | solution.py:323
  28.5 0.0 collective-permute-done.other
  28.5 3.1 %stack_and_slant.1 = bf16[1024,128]{1,0:T(8,128)(2,1)S(1)} custom-call(bf16[2048,128]{1,0:T(8,128)(2,1)S(1)} %bitcast.6, bf16[4,512,128]{2,1,0:T(8,128)(2,1)S(1)} %get-tuple-element.12.own, bf16[4,512,128]{2,1,0:T(8,128)(2,1)S(1)} %collective-permute-done.other, bf16[16,256,256]{2,1,0:T(8,128)(2,1)S(1)} %get-tuple-element.13.steep, ...), custom_call_target="tpu_custom_call" | custom-call | tf_op jit(solution)/shard_map/stack_and_slant/pallas_call | solution.py:325
  31.6 15.0 %all_to_all.11 = bf16[128,8,128]{2,1,0:T(8,128)(2,1)S(1)} all-to-all(bf16[128,8,128]{2,1,0:T(8,128)(2,1)S(1)} %bitcast.7), channel_id=1, replica_groups=mesh['days'=2,'chan'=64] {'days','chan'}, dimensions={0} | all-to-all | bytes 524288 | tf_op jit(solution)/shard_map/all_to_all | solution.py:338
  46.6 0.6 %sum.1 = f32[2,2,2,256]{3,2,1,0:T(2,128)} custom-call(bf16[1024,128]{1,0:T(8,128)(2,1)S(1)} %bitcast.8), custom_call_target="tpu_custom_call" | custom-call | tf_op jit(solution)/shard_map/sum/pallas_call | solution.py:339
Async XLA Ops:
  0.0 28.5 %collective-permute-start = (bf16[4,512,128]{2,1,0:T(8,128)(2,1)}, bf16[4,512,128]{2,1,0:T(8,128)(2,1)S(1)}, u32[]{:S(2)}, u32[]{:S(2)}) collective-permute-start(bf16[4,512,128]{2,1,0:T(8,128)(2,1)} %spectra.1), channel_id=1, source_target_pairs={{0,64},{64,0},{1,65},{65,1},{2,66},{66,2},{3,67},{67,3},{4,68},{68... | collective-permute-start | bytes 1572872 | tf_op jit(solution)/shard_map/ppermute | solution.py:294
